TPU v7x, 32 devices: a whole 2x2x4 slice. The times are simulated.
32 devices in a mesh: row: 4 (over y, x), col: 4 (over z), rep: 2 (over core).
Axes of the slice: x: 2, y: 2, z: 4, core: 2. Of those that a mesh axis runs over, the one named last changes fastest.
Arguments:
- features: bfloat16 [2, 2048, 512], P('rep', ('row', 'col')), may hold values from -6 to 6
- cotangent: bfloat16 [2, 2048, 512], P('rep', ('row', 'col')), may hold values from -6 to 6
- weight: bfloat16 [512, 512], replicated, may hold values from -0.25 to 0.25
- tile_values: bfloat16 [2, 256, 128, 128], P('rep', ('row', 'col')), may hold values from -0.25 to 0.25
- tile_out: int32 [2, 256], P('rep', ('row', 'col')), may hold values from 0 to 3
- tile_in: int32 [2, 256], P('rep', ('row', 'col')), may hold values from 0 to 3
- tile_count: int32 [2, 16], P('rep', ('row', 'col')), may hold values from 8 to 16, as said below
Outputs:
- out_feats: bfloat16 [2, 2048, 512], P('rep', ('row', 'col'))
- grad_feats: bfloat16 [2, 2048, 512], P('rep', ('row', 'col'))
- grad_weight: float32 [512, 512], replicated
Inputs may be any that keep to these rules, and one draw needn't show every extreme that they name: `tile_count`: in each window some group has all 16 slots live.
All inputs are finite; a program needn't handle non-finite values.
Results may differ from a plain program's by a relative error of at most 0.015.
Values may be sent and summed in bfloat16 or wider, within the bound.
A program may use at most 64 MiB of HBM per device.

v0:
```python
import jax
import jax.numpy as jnp
from jax import lax
from jax.sharding import PartitionSpec as P

SECTIONS = 4


def passed_along(value, axis, steps):
    count = lax.axis_size(axis)
    leading, last = (max(0, -steps), min(count, count - steps))
    return lax.ppermute(value, axis, [(source, source + steps) for source in range(leading, last)])


def body(features, cotangent, weight, tile_values, tile_out, tile_in, tile_count):
    field_in = features[0]
    values = tile_values[0]
    outs_idx = tile_out[0]
    ins_idx = tile_in[0]
    count = tile_count[0, 0]
    node_rows, width = field_in.shape
    edge = values.shape[-1]
    per_span = node_rows // edge
    half = SECTIONS // 2
    col_count = lax.axis_size("col")
    out_count = col_count * per_span
    in_count = SECTIONS * per_span
    slot_total = values.shape[0]
    live = (jnp.arange(slot_total, dtype=jnp.int32) < count).astype(jnp.float32)
    out_hot = (outs_idx[None, :] == jnp.arange(out_count, dtype=jnp.int32)[:, None]).astype(
        jnp.float32
    ) * live[None, :]
    in_hot = (ins_idx[None, :] == jnp.arange(in_count, dtype=jnp.int32)[:, None]).astype(
        jnp.float32
    ) * live[None, :]
    pieces = []
    for section in range(SECTIONS):
        offset = section - half
        if offset == 0:
            pieces.append(field_in)
        else:
            pieces.append(passed_along(field_in, "row", -offset))
    blocks = jnp.stack(pieces)
    picked = blocks[ins_idx]
    prods = jnp.einsum("tij,tjf->tif", values, picked, preferred_element_type=jnp.float32)
    part = jnp.einsum("ot,tif->oif", out_hot, prods, precision=lax.Precision.HIGHEST)
    summed = lax.psum_scatter(
        part.reshape(out_count * edge, width).astype(jnp.bfloat16),
        "col",
        scatter_dimension=0,
        tiled=True,
    )
    pre = jnp.dot(summed, weight, preferred_element_type=jnp.float32)
    out_feats = jax.nn.silu(pre).astype(jnp.bfloat16)
    sigma = jax.nn.sigmoid(pre)
    dpre = (cotangent[0].astype(jnp.float32) * sigma * (1.0 + pre * (1.0 - sigma))).astype(
        jnp.bfloat16
    )
    local_grad = jnp.einsum("nf,ng->fg", summed, dpre, preferred_element_type=jnp.float32)
    total_nodes = node_rows * lax.axis_size("row") * col_count * lax.axis_size("rep")
    grad_weight = lax.psum(local_grad, ("row", "col", "rep")) * jnp.float32(total_nodes) ** (-0.5)
    dhidden = jnp.einsum("nf,gf->ng", dpre, weight, preferred_element_type=jnp.float32).astype(
        jnp.bfloat16
    )
    row_grads = lax.all_gather(dhidden, "col", axis=0, tiled=True).reshape(out_count, edge, width)
    chosen = row_grads[outs_idx]
    back_prods = jnp.einsum("tij,tif->tjf", values, chosen, preferred_element_type=jnp.float32)
    sections_part = jnp.einsum("it,tjf->ijf", in_hot, back_prods, precision=lax.Precision.HIGHEST)
    sections_part = sections_part.astype(jnp.bfloat16)
    total = jnp.zeros((node_rows, width), jnp.float32)
    for section in range(SECTIONS):
        offset = section - half
        if offset == 0:
            arrived = sections_part[section]
        else:
            arrived = passed_along(sections_part[section], "row", offset)
        total = total + arrived.astype(jnp.float32)
    grad_feats = total.astype(jnp.bfloat16)
    return (out_feats[None], grad_feats[None], grad_weight)


def solution(mesh):
    return jax.shard_map(
        body,
        mesh=mesh,
        in_specs=(
            P("rep", ("row", "col"), None),
            P("rep", ("row", "col"), None),
            P(),
            P("rep", ("row", "col"), None, None),
            P("rep", ("row", "col")),
            P("rep", ("row", "col")),
            P("rep", ("row", "col")),
        ),
        out_specs=(P("rep", ("row", "col"), None), P("rep", ("row", "col"), None), P()),
        check_vma=False,
    )
```

profile of v0, /device:TPU:0, one launch (start us, length us, event | category | flops | bytes accessed | tf_op | source)
XLA Modules:
  0.0 224.5 jit_solution(10835809086337116893)
XLA Ops:
  7.2 5.0 %collective-permute-start = (bf16[128,512]{1,0:T(8,128)(2,1)}, bf16[128,512]{1,0:T(8,128)(2,1)S(1)}, u32[]{:S(2)}, u32[]{:S(2)}) collective-permute-start(bf16[128,512]{1,0:T(8,128)(2,1)} %bitcast.76), channel_id=1, source_target_pairs={{0,16},{8,24},{1,17},{9,25},{2,18},{10,26},{3,19},{11,27},{4,20},{... | collective-permute-start | bytes 393224 | tf_op jit(solution)/shard_map/ppermute | solution.py:12
  12.2 3.4 %collective-permute-start.1 = (bf16[128,512]{1,0:T(8,128)(2,1)}, bf16[128,512]{1,0:T(8,128)(2,1)S(1)}, u32[]{:S(2)}, u32[]{:S(2)}) collective-permute-start(bf16[128,512]{1,0:T(8,128)(2,1)} %bitcast.77), channel_id=1, source_target_pairs={{0,8},{8,16},{16,24},{1,9},{9,17},{17,25},{2,10},{10,18},{18,26},{... | collective-permute-start | bytes 393224 | tf_op jit(solution)/shard_map/ppermute | solution.py:12
  15.7 1.3 collective-permute-start.2
  17.0 0.7 fusion.30
  18.3 0.2 collective-permute-done.1
  18.5 4.3 %collective-permute-done.2 = bf16[128,512]{1,0:T(8,128)(2,1)S(1)} collective-permute-done((bf16[128,512]{1,0:T(8,128)(2,1)}, bf16[128,512]{1,0:T(8,128)(2,1)S(1)}, u32[]{:S(2)}, u32[]{:S(2)}) %collective-permute-start.2) | collective-permute-done | bytes 131104 | tf_op jit(solution)/shard_map/ppermute | solution.py:12
  22.7 1.0 pad_maximum_fusion
  23.7 0.7 gather_fusion
  24.4 2.7 %fusion.12 = f32[16,512,128]{2,1,0:T(8,128)} fusion(bf16[16,128,512]{2,1,0:T(8,128)(2,1)S(1)} %gather_fusion, bf16[1,16,128,128]{3,2,1,0:T(8,128)(2,1)S(1)} %copy-done), kind=kOutput, calls=%fused_computation.12 | convolution fusion | flops 268435456 | bytes 6815744 | tf_op jit(solution)/shard_map/tij,tjf->tif/dot_general | solution.py:45
  27.1 5.5 %copy.16 = f32[16,512,128]{1,0,2:T(8,128)} copy(f32[16,512,128]{2,1,0:T(8,128)} %fusion.12) | data formatting | bytes 8388608 | tf_op jit(solution)/shard_map/tij,tjf->tif/dot_general | solution.py:45
  32.6 4.3 %fusion.4 = bf16[4,128,512]{2,0,1:T(4,128)(2,1)S(1)} fusion(f32[16,512,128]{1,0,2:T(8,128)} %copy.16, f32[16]{0:T(128)S(1)} %compare_convert_fusion, s32[16]{0:T(128)S(1)} %bitcast.82), kind=kOutput, calls=%fused_computation.6 | convolution fusion | flops 50593920 | bytes 4718720 | tf_op jit(solution)/shard_map/ot,tif->oif/dot_general | solution.py:46
  37.0 0.9 copy.13
  37.9 0.0 all-reduce.2.cloned.1.call-start
  38.0 21.4 %reduce-scatter.2.cloned.1.call-done = bf16[128,512]{1,0:T(8,128)(2,1)} async-done(((bf16[512,512]{1,0:T(8,128)(2,1)}), bf16[128,512]{1,0:T(8,128)(2,1)}) %reduce-scatter.2.cloned.1.call-update) | async-done | bytes 131088 | tf_op jit(solution)/shard_map/reduce_scatter | solution.py:47
  59.4 1.1 fusion.38
  60.6 0.3 convolution_convert_fusion
  60.9 15.9 %all_gather.3 = bf16[512,512]{1,0:T(8,128)(2,1)S(1)} all-gather(bf16[128,512]{1,0:T(8,128)(2,1)S(1)} %convolution_convert_fusion), channel_id=1, replica_groups=mesh['row'=4,'col'=4,'rep'=2] {'col'}, dimensions={0}, use_global_device_ids=true | all-gather | bytes 655360 | tf_op jit(solution)/shard_map/all_gather | solution.py:65
  76.7 0.7 gather_fusion.1
  77.4 2.8 %fusion.10 = f32[16,512,128]{2,1,0:T(8,128)} fusion(bf16[16,128,512]{2,1,0:T(8,128)(2,1)S(1)} %gather_fusion.1, bf16[1,16,128,128]{3,2,1,0:T(8,128)(2,1)S(1)} %copy-done), kind=kOutput, calls=%fused_computation.10 | convolution fusion | flops 268435456 | bytes 6815744 | tf_op jit(solution)/shard_map/tij,tif->tjf/dot_general | solution.py:67
  80.2 5.5 %copy.17 = f32[16,512,128]{1,0,2:T(8,128)} copy(f32[16,512,128]{2,1,0:T(8,128)} %fusion.10) | data formatting | bytes 8388608 | tf_op jit(solution)/shard_map/tij,tif->tjf/dot_general | solution.py:67
  85.7 1.4 fusion.34
  87.1 4.3 %fusion.7 = bf16[4,128,512]{2,0,1:T(4,128)(2,1)S(1)} fusion(f32[16,512,128]{1,0,2:T(8,128)} %copy.17, s32[16]{0:T(128)S(1)} %bitcast.83, f32[16]{0:T(128)S(1)} %compare_convert_fusion), kind=kOutput, calls=%fused_computation.7 | convolution fusion | flops 50593920 | bytes 4718720 | tf_op jit(solution)/shard_map/it,tjf->ijf/dot_general | solution.py:68
  91.4 0.7 fusion.37
  92.1 1.3 collective-permute-start.3
  93.5 1.3 collective-permute-start.4
  94.8 4.6 %collective-permute-start.5 = (bf16[128,512]{1,0:T(8,128)(2,1)S(1)}, bf16[128,512]{1,0:T(8,128)(2,1)S(1)}, u32[]{:S(2)}, u32[]{:S(2)}) collective-permute-start(bf16[128,512]{1,0:T(8,128)(2,1)S(1)} %bitcast.75), channel_id=1, source_target_pairs={{0,8},{8,16},{16,24},{1,9},{9,17},{17,25},{2,10},{10,18},{18,26},{... | collective-permute-start | bytes 393224 | tf_op jit(solution)/shard_map/ppermute | solution.py:12
  99.4 0.7 fusion.19
  100.1 0.2 collective-permute-done.4
  100.3 1.7 collective-permute-done.5
  102.0 0.7 fusion.18
  102.7 112.6 %all-reduce.2.cloned.1.call-done = f32[512,512]{1,0:T(8,128)} async-done(((f32[512,512]{1,0:T(8,128)}), f32[512,512]{1,0:T(8,128)}) %all-reduce.2.cloned.1.call-update) | async-done | bytes 1048592 | tf_op jit(solution)/shard_map/psum | solution.py:61
  215.3 2.3 %broadcast_multiply_fusion = f32[512,512]{1,0:T(8,128)} fusion(f32[512,512]{1,0:T(8,128)} %all-reduce.2.cloned.1.call-done), kind=kLoop, calls=%fused_computation.14 | loop fusion | flops 262144 | bytes 2097152 | tf_op jit(solution)/shard_map/mul | solution.py:61
  (24 shorter events, 0.2 us)
Async XLA Ops:
  7.2 17.2 %copy-start = (bf16[1,16,128,128]{3,2,1,0:T(8,128)(2,1)S(1)}, bf16[1,16,128,128]{3,2,1,0:T(8,128)(2,1)}, u32[]{:S(2)}) copy-start(bf16[1,16,128,128]{3,2,1,0:T(8,128)(2,1)} %param.10) | copy-start | bytes 1572868
  7.2 52.2 %reduce-scatter.2.cloned.1.call-start = ((), (), s32[]{:S(2)}) async-start(), calls=%async_computation.1 | async-start | bytes 655360 | tf_op jit(solution)/shard_map/reduce_scatter | solution.py:47
  7.2 11.1 %collective-permute-start = (bf16[128,512]{1,0:T(8,128)(2,1)}, bf16[128,512]{1,0:T(8,128)(2,1)S(1)}, u32[]{:S(2)}, u32[]{:S(2)}) collective-permute-start(bf16[128,512]{1,0:T(8,128)(2,1)} %bitcast.76), channel_id=1, source_target_pairs={{0,16},{8,24},{1,17},{9,25},{2,18},{10,26},{3,19},{11,27},{4,20},{... | collective-permute-start | bytes 393224 | tf_op jit(solution)/shard_map/ppermute | solution.py:12
  12.2 6.2 %collective-permute-start.1 = (bf16[128,512]{1,0:T(8,128)(2,1)}, bf16[128,512]{1,0:T(8,128)(2,1)S(1)}, u32[]{:S(2)}, u32[]{:S(2)}) collective-permute-start(bf16[128,512]{1,0:T(8,128)(2,1)} %bitcast.77), channel_id=1, source_target_pairs={{0,8},{8,16},{16,24},{1,9},{9,17},{17,25},{2,10},{10,18},{18,26},{... | collective-permute-start | bytes 393224 | tf_op jit(solution)/shard_map/ppermute | solution.py:12
  15.7 7.1 %collective-permute-start.2 = (bf16[128,512]{1,0:T(8,128)(2,1)}, bf16[128,512]{1,0:T(8,128)(2,1)S(1)}, u32[]{:S(2)}, u32[]{:S(2)}) collective-permute-start(bf16[128,512]{1,0:T(8,128)(2,1)} %bitcast.78), channel_id=1, source_target_pairs={{8,0},{16,8},{24,16},{9,1},{17,9},{25,17},{10,2},{18,10},{26,18},{... | collective-permute-start | bytes 393224 | tf_op jit(solution)/shard_map/ppermute | solution.py:12
  27.1 5.5 %copy-start.3 = (s32[1,16]{1,0:T(1,128)S(1)}, s32[1,16]{1,0:T(1,128)}, u32[]{:S(2)}) copy-start(s32[1,16]{1,0:T(1,128)} %param.11) | copy-start | bytes 196
  32.6 26.8 %copy-start.1 = (bf16[512,512]{1,0:T(8,128)(2,1)S(1)}, bf16[512,512]{1,0:T(8,128)(2,1)}, u32[]{:S(2)}) copy-start(bf16[512,512]{1,0:T(8,128)(2,1)} %param.9) | copy-start | bytes 1572868
  37.0 23.6 %copy-start.5 = (bf16[1,128,512]{2,1,0:T(8,128)(2,1)S(1)}, bf16[1,128,512]{2,1,0:T(8,128)(2,1)}, u32[]{:S(2)}) copy-start(bf16[1,128,512]{2,1,0:T(8,128)(2,1)} %param.8) | copy-start | bytes 393220
  37.9 177.4 %all-reduce.2.cloned.1.call-start = ((), (), s32[]{:S(2)}) async-start(), calls=%async_computation.2 | async-start | bytes 2097152 | tf_op jit(solution)/shard_map/psum | solution.py:61
  80.2 5.5 %copy-start.2 = (bf16[128,512]{1,0:T(8,128)(2,1)S(1)}, bf16[128,512]{1,0:T(8,128)(2,1)}, u32[]{:S(2)}) copy-start(bf16[128,512]{1,0:T(8,128)(2,1)} %reduce-scatter.2.cloned.1.call-done) | copy-start | bytes 393220
  85.7 1.4 copy-start.4
  92.1 8.0 %collective-permute-start.3 = (bf16[128,512]{1,0:T(8,128)(2,1)S(1)}, bf16[128,512]{1,0:T(8,128)(2,1)S(1)}, u32[]{:S(2)}, u32[]{:S(2)}) collective-permute-start(bf16[128,512]{1,0:T(8,128)(2,1)S(1)} %bitcast.73), channel_id=1, source_target_pairs={{16,0},{24,8},{17,1},{25,9},{18,2},{26,10},{19,3},{27,11},{20,4},{... | collective-permute-start | bytes 393224 | tf_op jit(solution)/shard_map/ppermute | solution.py:12
  93.5 6.9 %collective-permute-start.4 = (bf16[128,512]{1,0:T(8,128)(2,1)S(1)}, bf16[128,512]{1,0:T(8,128)(2,1)S(1)}, u32[]{:S(2)}, u32[]{:S(2)}) collective-permute-start(bf16[128,512]{1,0:T(8,128)(2,1)S(1)} %bitcast.74), channel_id=1, source_target_pairs={{8,0},{16,8},{24,16},{9,1},{17,9},{25,17},{10,2},{18,10},{26,18},{... | collective-permute-start | bytes 393224 | tf_op jit(solution)/shard_map/ppermute | solution.py:12
  94.8 7.2 %collective-permute-start.5 = (bf16[128,512]{1,0:T(8,128)(2,1)S(1)}, bf16[128,512]{1,0:T(8,128)(2,1)S(1)}, u32[]{:S(2)}, u32[]{:S(2)}) collective-permute-start(bf16[128,512]{1,0:T(8,128)(2,1)S(1)} %bitcast.75), channel_id=1, source_target_pairs={{0,8},{8,16},{16,24},{1,9},{9,17},{17,25},{2,10},{10,18},{18,26},{... | collective-permute-start | bytes 393224 | tf_op jit(solution)/shard_map/ppermute | solution.py:12
Sparse Core Ops, SparseCore 0:
  38.0 21.3 reduce-scatter.1
  87.2 128.0 all-reduce.1
where the time goes:
time: 225 us; the launch traced here: 224 us
  waiting for transfers between devices  140 us (62%)
  starting transfers between devices  16.9 us (8%)
  matrix products  16.9 us (8%)
  blocking collectives  15.9 us (7%)
  between operations  14.9 us (7%)
  local copies, waits for them, and re-layouts  13.4 us (6%)
  other arithmetic  6.11 us (3%)
    psum x1, waiting for transfers between devices, body(): lax.psum(local_grad, ('row', 'col', 'rep'))  113 us
    reduce_scatter x1, waiting for transfers between devices, body(): lax.psum_scatter(part.reshape(out_count * edge, width).astype(jnp.bfloat1...  21.4 us
    ppermute x6, starting transfers between devices, passed_along(): lax.ppermute(value, axis, [(source, source + steps) for source in range(l...  16.8 us
    all_gather x1, blocking collectives, body(): lax.all_gather(dhidden, 'col', axis=0, tiled=True)  15.9 us
    ppermute x6, waiting for transfers between devices, passed_along(): lax.ppermute(value, axis, [(source, source + steps) for source in range(l...  6.33 us
    dot_general x1, local copies, waits for them, and re-layouts, body(): jnp.einsum('tij,tif->tjf', values, chosen, preferred_element_type=jnp.flo...  5.54 us
    dot_general x1, local copies, waits for them, and re-layouts, body(): jnp.einsum('tij,tjf->tif', values, picked, preferred_element_type=jnp.flo...  5.51 us
  transfers between devices with their start and end apart: 8, of which 6 were waited for; matrix products, arithmetic and copies ran while one was open for 3% of the time, Pallas kernels for 0%

commit v1 on v0

--- a/solution.py
+++ b/solution.py
@@ -4,6 +4,18 @@
 from jax.sharding import PartitionSpec as P
 
 SECTIONS = 4
+
+
+def doubled_up(shard, axis, dim):
+    ways, here = (lax.axis_size(axis), lax.axis_index(axis))
+    grown, reach = (shard, 1)
+    while reach < ways:
+        theirs = lax.ppermute(grown, axis, [(d, d ^ reach) for d in range(ways)])
+        mine_first = jnp.concatenate([grown, theirs], axis=dim)
+        theirs_first = jnp.concatenate([theirs, grown], axis=dim)
+        grown = jnp.where(here & reach == 0, mine_first, theirs_first)
+        reach = 2 * reach
+    return grown
 
 
 def passed_along(value, axis, steps):
@@ -62,7 +74,7 @@
     dhidden = jnp.einsum("nf,gf->ng", dpre, weight, preferred_element_type=jnp.float32).astype(
         jnp.bfloat16
     )
-    row_grads = lax.all_gather(dhidden, "col", axis=0, tiled=True).reshape(out_count, edge, width)
+    row_grads = doubled_up(dhidden, "col", 0).reshape(out_count, edge, width)
     chosen = row_grads[outs_idx]
     back_prods = jnp.einsum("tij,tif->tjf", values, chosen, preferred_element_type=jnp.float32)
     sections_part = jnp.einsum("it,tjf->ijf", in_hot, back_prods, precision=lax.Precision.HIGHEST)

time: 225 us -> 208 us (0.924)
  blocking collectives: 15.9 us -> 0 us
    all_gather x1 -> x0, blocking collectives: 15.9 us -> none  [body(): lax.all_gather(dhidden, 'col', axis=0, tiled=True)]
    psum x1, waiting for transfers between devices: 113 us -> 98.2 us  [body(): lax.psum(local_grad, ('row', 'col', 'rep'))]
    ppermute x0 -> x2, waiting for transfers between devices: none -> 14.2 us  [doubled_up(): theirs = lax.ppermute(grown, axis, [(d, d ^ reach) for d in range(ways)])]
  transfers between devices with their start and end apart: 8 -> 10, of which waited for: 6 -> 6; matrix products, arithmetic and copies ran while one was open for 3% -> 9% of each run, Pallas kernels for 0% -> 0%
where the time goes in v1:
time: 208 us
  waiting for transfers between devices  138 us (66%)
  starting transfers between devices  17.8 us (9%)
  matrix products  17 us (8%)
  between operations  14.9 us (7%)
  local copies, waits for them, and re-layouts  13.4 us (6%)
  other arithmetic  6.38 us (3%)
    psum x1, waiting for transfers between devices, body(): lax.psum(local_grad, ('row', 'col', 'rep'))  98.2 us
    reduce_scatter x1, waiting for transfers between devices, body(): lax.psum_scatter(part.reshape(out_count * edge, width).astype(jnp.bfloat1...  21.4 us
    ppermute x6, starting transfers between devices, passed_along(): lax.ppermute(value, axis, [(source, source + steps) for source in range(l...  16.8 us
    ppermute x2, waiting for transfers between devices, doubled_up(): theirs = lax.ppermute(grown, axis, [(d, d ^ reach) for d in range(ways)])  14.2 us
    dot_general x1, local copies, waits for them, and re-layouts, body(): jnp.einsum('tij,tif->tjf', values, chosen, preferred_element_type=jnp.flo...  5.53 us
    dot_general x1, local copies, waits for them, and re-layouts, body(): jnp.einsum('tij,tjf->tif', values, picked, preferred_element_type=jnp.flo...  5.51 us
    ppermute x6, waiting for transfers between devices, passed_along(): lax.ppermute(value, axis, [(source, source + steps) for source in range(l...  4.44 us
    dot_general x1, matrix products, body(): jnp.einsum('ot,tif->oif', out_hot, prods, precision=lax.Precision.HIGHEST)  4.34 us
  transfers between devices with their start and end apart: 10, of which 6 were waited for; matrix products, arithmetic and copies ran while one was open for 9% of the time, Pallas kernels for 0%

profile of v1, /device:TPU:0, one launch (start us, length us, event | category | flops | bytes accessed | tf_op | source)
XLA Modules:
  0.0 207.8 jit_solution(5129480842648217826)
XLA Ops:
  7.2 5.0 %collective-permute-start = (bf16[128,512]{1,0:T(8,128)(2,1)}, bf16[128,512]{1,0:T(8,128)(2,1)S(1)}, u32[]{:S(2)}, u32[]{:S(2)}) collective-permute-start(bf16[128,512]{1,0:T(8,128)(2,1)} %bitcast.76), channel_id=1, source_target_pairs={{0,16},{8,24},{1,17},{9,25},{2,18},{10,26},{3,19},{11,27},{4,20},{... | collective-permute-start | bytes 393224 | tf_op jit(solution)/shard_map/ppermute | solution.py:24
  12.2 3.4 %collective-permute-start.1 = (bf16[128,512]{1,0:T(8,128)(2,1)}, bf16[128,512]{1,0:T(8,128)(2,1)S(1)}, u32[]{:S(2)}, u32[]{:S(2)}) collective-permute-start(bf16[128,512]{1,0:T(8,128)(2,1)} %bitcast.77), channel_id=1, source_target_pairs={{0,8},{8,16},{16,24},{1,9},{9,17},{17,25},{2,10},{10,18},{18,26},{... | collective-permute-start | bytes 393224 | tf_op jit(solution)/shard_map/ppermute | solution.py:24
  15.7 1.3 collective-permute-start.2
  17.0 0.7 fusion.30
  18.3 0.2 collective-permute-done.1
  18.5 4.3 %collective-permute-done.2 = bf16[128,512]{1,0:T(8,128)(2,1)S(1)} collective-permute-done((bf16[128,512]{1,0:T(8,128)(2,1)}, bf16[128,512]{1,0:T(8,128)(2,1)S(1)}, u32[]{:S(2)}, u32[]{:S(2)}) %collective-permute-start.2) | collective-permute-done | bytes 131104 | tf_op jit(solution)/shard_map/ppermute | solution.py:24
  22.7 1.0 pad_maximum_fusion
  23.7 0.7 gather_fusion
  24.4 2.7 %fusion.12 = f32[16,512,128]{2,1,0:T(8,128)} fusion(bf16[16,128,512]{2,1,0:T(8,128)(2,1)S(1)} %gather_fusion, bf16[1,16,128,128]{3,2,1,0:T(8,128)(2,1)S(1)} %copy-done), kind=kOutput, calls=%fused_computation.13 | convolution fusion | flops 268435456 | bytes 6815744 | tf_op jit(solution)/shard_map/tij,tjf->tif/dot_general | solution.py:57
  27.1 5.5 %copy.16 = f32[16,512,128]{1,0,2:T(8,128)} copy(f32[16,512,128]{2,1,0:T(8,128)} %fusion.12) | data formatting | bytes 8388608 | tf_op jit(solution)/shard_map/tij,tjf->tif/dot_general | solution.py:57
  32.7 4.3 %fusion.4 = bf16[4,128,512]{2,0,1:T(4,128)(2,1)S(1)} fusion(f32[16,512,128]{1,0,2:T(8,128)} %copy.16, f32[16]{0:T(128)S(1)} %compare_convert_fusion, s32[16]{0:T(128)S(1)} %bitcast.82), kind=kOutput, calls=%fused_computation.6 | convolution fusion | flops 50593920 | bytes 4718720 | tf_op jit(solution)/shard_map/ot,tif->oif/dot_general | solution.py:58
  37.0 0.9 copy.13
  38.0 21.4 %reduce-scatter.2.cloned.1.call-done = bf16[128,512]{1,0:T(8,128)(2,1)} async-done(((bf16[512,512]{1,0:T(8,128)(2,1)}), bf16[128,512]{1,0:T(8,128)(2,1)}) %reduce-scatter.2.cloned.1.call-update) | async-done | bytes 131088 | tf_op jit(solution)/shard_map/reduce_scatter | solution.py:59
  59.4 1.2 fusion.38
  60.6 0.3 convolution_convert_fusion
  61.1 4.9 %collective-permute-done.3 = bf16[128,512]{1,0:T(8,128)(2,1)S(1)} collective-permute-done((bf16[128,512]{1,0:T(8,128)(2,1)S(1)}, bf16[128,512]{1,0:T(8,128)(2,1)S(1)}, u32[]{:S(2)}, u32[]{:S(2)}) %collective-permute-start.3) | collective-permute-done | bytes 131104 | tf_op jit(solution)/shard_map/ppermute | solution.py:13
  66.0 0.8 collective-permute-start.4
  66.9 1.3 fusion.34
  68.2 0.7 fusion.19
  69.0 9.3 %collective-permute-done.4 = bf16[256,512]{1,0:T(8,128)(2,1)S(1)} collective-permute-done((bf16[256,512]{1,0:T(8,128)(2,1)S(1)}, bf16[256,512]{1,0:T(8,128)(2,1)S(1)}, u32[]{:S(2)}, u32[]{:S(2)}) %collective-permute-start.4) | collective-permute-done | bytes 262176 | tf_op jit(solution)/shard_map/ppermute | solution.py:13
  78.3 0.2 maximum_select_fusion
  78.5 0.7 gather_fusion.1
  79.2 2.7 %fusion.10 = f32[16,512,128]{2,1,0:T(8,128)} fusion(bf16[16,128,512]{2,1,0:T(8,128)(2,1)S(1)} %gather_fusion.1, bf16[1,16,128,128]{3,2,1,0:T(8,128)(2,1)S(1)} %copy-done), kind=kOutput, calls=%fused_computation.11 | convolution fusion | flops 268435456 | bytes 6815744 | tf_op jit(solution)/shard_map/tij,tif->tjf/dot_general | solution.py:79
  81.9 5.5 %copy.17 = f32[16,512,128]{1,0,2:T(8,128)} copy(f32[16,512,128]{2,1,0:T(8,128)} %fusion.10) | data formatting | bytes 8388608 | tf_op jit(solution)/shard_map/tij,tif->tjf/dot_general | solution.py:79
  87.4 4.3 %fusion.7 = bf16[4,128,512]{2,0,1:T(4,128)(2,1)S(1)} fusion(f32[16,512,128]{1,0,2:T(8,128)} %copy.17, s32[16]{0:T(128)S(1)} %bitcast.83, f32[16]{0:T(128)S(1)} %compare_convert_fusion), kind=kOutput, calls=%fused_computation.7 | convolution fusion | flops 50593920 | bytes 4718720 | tf_op jit(solution)/shard_map/it,tjf->ijf/dot_general | solution.py:80
  91.7 0.7 fusion.37
  92.5 1.3 collective-permute-start.5
  93.8 1.3 collective-permute-start.6
  95.2 4.6 %collective-permute-start.7 = (bf16[128,512]{1,0:T(8,128)(2,1)S(1)}, bf16[128,512]{1,0:T(8,128)(2,1)S(1)}, u32[]{:S(2)}, u32[]{:S(2)}) collective-permute-start(bf16[128,512]{1,0:T(8,128)(2,1)S(1)} %bitcast.75), channel_id=1, source_target_pairs={{0,8},{8,16},{16,24},{1,9},{9,17},{17,25},{2,10},{10,18},{18,26},{... | collective-permute-start | bytes 393224 | tf_op jit(solution)/shard_map/ppermute | solution.py:24
  99.7 98.2 %all-reduce.2.cloned.1.call-done = f32[512,512]{1,0:T(8,128)} async-done(((f32[512,512]{1,0:T(8,128)}), f32[512,512]{1,0:T(8,128)}) %all-reduce.2.cloned.1.call-update) | async-done | bytes 1048592 | tf_op jit(solution)/shard_map/psum | solution.py:73
  197.9 2.3 %broadcast_multiply_fusion = f32[512,512]{1,0:T(8,128)} fusion(f32[512,512]{1,0:T(8,128)} %all-reduce.2.cloned.1.call-done), kind=kLoop, calls=%fused_computation.15 | loop fusion | flops 262144 | bytes 2097152 | tf_op jit(solution)/shard_map/mul | solution.py:73
  200.2 0.7 fusion.18
  (29 shorter events, 0.4 us)
Async XLA Ops:
  7.2 17.2 %copy-start = (bf16[1,16,128,128]{3,2,1,0:T(8,128)(2,1)S(1)}, bf16[1,16,128,128]{3,2,1,0:T(8,128)(2,1)}, u32[]{:S(2)}) copy-start(bf16[1,16,128,128]{3,2,1,0:T(8,128)(2,1)} %param.10) | copy-start | bytes 1572868
  7.2 52.2 %reduce-scatter.2.cloned.1.call-start = ((), (), s32[]{:S(2)}) async-start(), calls=%async_computation.1 | async-start | bytes 655360 | tf_op jit(solution)/shard_map/reduce_scatter | solution.py:59
  7.2 11.1 %collective-permute-start = (bf16[128,512]{1,0:T(8,128)(2,1)}, bf16[128,512]{1,0:T(8,128)(2,1)S(1)}, u32[]{:S(2)}, u32[]{:S(2)}) collective-permute-start(bf16[128,512]{1,0:T(8,128)(2,1)} %bitcast.76), channel_id=1, source_target_pairs={{0,16},{8,24},{1,17},{9,25},{2,18},{10,26},{3,19},{11,27},{4,20},{... | collective-permute-start | bytes 393224 | tf_op jit(solution)/shard_map/ppermute | solution.py:24
  12.2 6.2 %collective-permute-start.1 = (bf16[128,512]{1,0:T(8,128)(2,1)}, bf16[128,512]{1,0:T(8,128)(2,1)S(1)}, u32[]{:S(2)}, u32[]{:S(2)}) collective-permute-start(bf16[128,512]{1,0:T(8,128)(2,1)} %bitcast.77), channel_id=1, source_target_pairs={{0,8},{8,16},{16,24},{1,9},{9,17},{17,25},{2,10},{10,18},{18,26},{... | collective-permute-start | bytes 393224 | tf_op jit(solution)/shard_map/ppermute | solution.py:24
  15.7 7.1 %collective-permute-start.2 = (bf16[128,512]{1,0:T(8,128)(2,1)}, bf16[128,512]{1,0:T(8,128)(2,1)S(1)}, u32[]{:S(2)}, u32[]{:S(2)}) collective-permute-start(bf16[128,512]{1,0:T(8,128)(2,1)} %bitcast.78), channel_id=1, source_target_pairs={{8,0},{16,8},{24,16},{9,1},{17,9},{25,17},{10,2},{18,10},{26,18},{... | collective-permute-start | bytes 393224 | tf_op jit(solution)/shard_map/ppermute | solution.py:24
  27.1 5.5 %copy-start.3 = (s32[1,16]{1,0:T(1,128)S(1)}, s32[1,16]{1,0:T(1,128)}, u32[]{:S(2)}) copy-start(s32[1,16]{1,0:T(1,128)} %param.11) | copy-start | bytes 196
  32.7 26.8 %copy-start.1 = (bf16[512,512]{1,0:T(8,128)(2,1)S(1)}, bf16[512,512]{1,0:T(8,128)(2,1)}, u32[]{:S(2)}) copy-start(bf16[512,512]{1,0:T(8,128)(2,1)} %param.9) | copy-start | bytes 1572868
  37.0 23.6 %copy-start.5 = (bf16[1,128,512]{2,1,0:T(8,128)(2,1)S(1)}, bf16[1,128,512]{2,1,0:T(8,128)(2,1)}, u32[]{:S(2)}) copy-start(bf16[1,128,512]{2,1,0:T(8,128)(2,1)} %param.8) | copy-start | bytes 393220
  37.9 160.0 %all-reduce.2.cloned.1.call-start = ((), (), s32[]{:S(2)}) async-start(), calls=%async_computation.2 | async-start | bytes 2097152 | tf_op jit(solution)/shard_map/psum | solution.py:73
  59.4 7.4 %copy-start.2 = (bf16[128,512]{1,0:T(8,128)(2,1)S(1)}, bf16[128,512]{1,0:T(8,128)(2,1)}, u32[]{:S(2)}) copy-start(bf16[128,512]{1,0:T(8,128)(2,1)} %reduce-scatter.2.cloned.1.call-done) | copy-start | bytes 393220
  60.9 5.0 %collective-permute-start.3 = (bf16[128,512]{1,0:T(8,128)(2,1)S(1)}, bf16[128,512]{1,0:T(8,128)(2,1)S(1)}, u32[]{:S(2)}, u32[]{:S(2)}) collective-permute-start(bf16[128,512]{1,0:T(8,128)(2,1)S(1)} %convolution_convert_fusion), channel_id=1, source_target_pairs={{0,2},{2,0},{4,6},{6,4},{1,3},{3,1},{5,7},{7,5},{8,10},{10,8},{12,... | collective-permute-start | bytes 393224 | tf_op jit(solution)/shard_map/ppermute | solution.py:13
  66.0 12.2 %collective-permute-start.4 = (bf16[256,512]{1,0:T(8,128)(2,1)S(1)}, bf16[256,512]{1,0:T(8,128)(2,1)S(1)}, u32[]{:S(2)}, u32[]{:S(2)}) collective-permute-start(bf16[256,512]{1,0:T(8,128)(2,1)S(1)} %maximum_select_fusion.1), channel_id=1, source_target_pairs={{0,4},{2,6},{4,0},{6,2},{1,5},{3,7},{5,1},{7,3},{8,12},{10,14},{12... | collective-permute-start | bytes 786440 | tf_op jit(solution)/shard_map/ppermute | solution.py:13
  81.9 5.5 %copy-start.4 = (s32[1,16]{1,0:T(1,128)S(1)}, s32[1,16]{1,0:T(1,128)}, u32[]{:S(2)}) copy-start(s32[1,16]{1,0:T(1,128)} %param.12) | copy-start | bytes 196
  92.5 107.7 %collective-permute-start.5 = (bf16[128,512]{1,0:T(8,128)(2,1)S(1)}, bf16[128,512]{1,0:T(8,128)(2,1)S(1)}, u32[]{:S(2)}, u32[]{:S(2)}) collective-permute-start(bf16[128,512]{1,0:T(8,128)(2,1)S(1)} %bitcast.73), channel_id=1, source_target_pairs={{16,0},{24,8},{17,1},{25,9},{18,2},{26,10},{19,3},{27,11},{20,4},{... | collective-permute-start | bytes 393224 | tf_op jit(solution)/shard_map/ppermute | solution.py:24
  93.8 106.4 %collective-permute-start.6 = (bf16[128,512]{1,0:T(8,128)(2,1)S(1)}, bf16[128,512]{1,0:T(8,128)(2,1)S(1)}, u32[]{:S(2)}, u32[]{:S(2)}) collective-permute-start(bf16[128,512]{1,0:T(8,128)(2,1)S(1)} %bitcast.74), channel_id=1, source_target_pairs={{8,0},{16,8},{24,16},{9,1},{17,9},{25,17},{10,2},{18,10},{26,18},{... | collective-permute-start | bytes 393224 | tf_op jit(solution)/shard_map/ppermute | solution.py:24
  95.2 105.1 %collective-permute-start.7 = (bf16[128,512]{1,0:T(8,128)(2,1)S(1)}, bf16[128,512]{1,0:T(8,128)(2,1)S(1)}, u32[]{:S(2)}, u32[]{:S(2)}) collective-permute-start(bf16[128,512]{1,0:T(8,128)(2,1)S(1)} %bitcast.75), channel_id=1, source_target_pairs={{0,8},{8,16},{16,24},{1,9},{9,17},{17,25},{2,10},{10,18},{18,26},{... | collective-permute-start | bytes 393224 | tf_op jit(solution)/shard_map/ppermute | solution.py:24
Sparse Core Ops, SparseCore 0:
  38.0 21.3 reduce-scatter.1
  68.3 129.5 all-reduce.1
